TPU v7x, 32 devices: a whole 2x2x4 slice. The times are simulated.
32 devices in a mesh: dp: 16 (over z, y, x), mp: 2 (over core).
Axes of the slice: x: 2, y: 2, z: 4, core: 2. Of those that a mesh axis runs over, the one named last changes fastest.
Arguments:
- tokens: bfloat16 [2, 96, 160, 768], P(None, ('dp', 'mp')), may hold values from -6 to 6
- lengths: int32 [2, 96], P(None, ('dp', 'mp')), may hold values from 95 to 160, as said below
- cotangent: bfloat16 [2, 96, 160, 768], P(None, ('dp', 'mp')), may hold values from -6 to 6
- attn_in: float32 [768, 3, 768], P('dp', None, 'mp')
- attn_out: float32 [768, 768], P('mp', 'dp')
- ffn_in: float32 [768, 3072], P('dp', 'mp')
- ffn_out: float32 [3072, 768], P('mp', 'dp')
- attn_in_first: float32 [768, 3, 768], P('dp', None, 'mp'), may hold values from -32 to 32
- attn_in_second: float32 [768, 3, 768], P('dp', None, 'mp'), may hold values from 2.7648 to 11.0592
- attn_out_first: float32 [768, 768], P('mp', 'dp'), may hold values from -56 to 56
- attn_out_second: float32 [768, 768], P('mp', 'dp'), may hold values from 7.68 to 30.72
- ffn_in_first: float32 [768, 3072], P('dp', 'mp'), may hold values from -56 to 56
- ffn_in_second: float32 [768, 3072], P('dp', 'mp'), may hold values from 7.68 to 30.72
- ffn_out_first: float32 [3072, 768], P('mp', 'dp'), may hold values from -64 to 64
- ffn_out_second: float32 [3072, 768], P('mp', 'dp'), may hold values from 11.0592 to 44.2368
- small: float32 [12, 768], replicated
- small_first: float32 [12, 768], replicated, may hold values from -56 to 56
- small_second: float32 [12, 768], replicated, may hold values from 7.68 to 30.72
Outputs:
- output: bfloat16 [2, 96, 160, 768], P(None, ('dp', 'mp'))
- tokens_grad: float32 [2, 96, 160, 768], P(None, ('dp', 'mp'))
- attn_in_grad: float32 [768, 3, 768], P('dp', None, 'mp')
- attn_in_first_new: float32 [768, 3, 768], P('dp', None, 'mp')
- attn_in_second_new: float32 [768, 3, 768], P('dp', None, 'mp')
- attn_in_new: float32 [768, 3, 768], P('dp', None, 'mp')
- attn_in_low: bfloat16 [768, 3, 768], P('dp', None, 'mp')
- attn_out_grad: float32 [768, 768], P('mp', 'dp')
- attn_out_first_new: float32 [768, 768], P('mp', 'dp')
- attn_out_second_new: float32 [768, 768], P('mp', 'dp')
- attn_out_new: float32 [768, 768], P('mp', 'dp')
- attn_out_low: bfloat16 [768, 768], P('mp', 'dp')
- ffn_in_grad: float32 [768, 3072], P('dp', 'mp')
- ffn_in_first_new: float32 [768, 3072], P('dp', 'mp')
- ffn_in_second_new: float32 [768, 3072], P('dp', 'mp')
- ffn_in_new: float32 [768, 3072], P('dp', 'mp')
- ffn_in_low: bfloat16 [768, 3072], P('dp', 'mp')
- ffn_out_grad: float32 [3072, 768], P('mp', 'dp')
- ffn_out_first_new: float32 [3072, 768], P('mp', 'dp')
- ffn_out_second_new: float32 [3072, 768], P('mp', 'dp')
- ffn_out_new: float32 [3072, 768], P('mp', 'dp')
- ffn_out_low: bfloat16 [3072, 768], P('mp', 'dp')
- small_grad: float32 [12, 768], replicated
- small_first_new: float32 [12, 768], replicated
- small_second_new: float32 [12, 768], replicated
- small_new: float32 [12, 768], replicated
- norms: float32 [2, 4], replicated
Inputs may be any that keep to these rules, and one draw needn't show every extreme that they name: `lengths`: true length of each chain; positions at or beyond it are padding; both ends of the range occur in every draw.
All inputs are finite; a program needn't handle non-finite values.
Results may differ from a plain program's by a relative error of at most 0.015.
The roundings to bfloat16 on the way count: a program that leaves them out, or rounds other values in their place, can miss the bound.
Values may be sent and summed in bfloat16 or wider, within the bound.
A program may use at most 192 MiB of HBM per device.

v0:
```python
import functools

import jax
import jax.numpy as jnp
from jax import lax
from jax.experimental import pallas as pl
from jax.experimental.pallas import tpu as pltpu
from jax.sharding import PartitionSpec as P

HEAD = 64
STEP = 10
NORM_EPS = 1e-05
RATE_MATRIX = 0.3
RATE_VECTOR = 0.2
BETA_FIRST = 0.9
BETA_SECOND = 0.999
ADAM_EPS = 1e-06
DECAY_RATE = 0.01
MASKED_SCORE = -1000000000.0

MESH = pl.DeviceIdType.MESH
bf16, f32 = jnp.bfloat16, jnp.float32
UNITS = 12
HALF = 384
MATRIX_OF = (0, 0, 0, 1, 2, 2, 2, 2, 3, 3, 3, 3)
WIDE = 768
LANES = 128
QUAD = 256
BLOCK = 192
G_SLOT = {2: 9, 1: 10, 0: 8}
PLANES, LINES, DIAGONAL, SIBLING, OWN, DONE, SHARDS = range(7)
SPLIT_GATHER = (5, 7, 9, 10)
SPLIT_SUMS = (8, 4, 9, 5)
GATHER = (
    ((PLANES, 0), (PLANES, 1), (PLANES, 2),),
    ((LINES, 0), (PLANES, 3), (LINES, 1), (PLANES, 4), (DIAGONAL, 0), (PLANES, 5), (LINES, 2), (PLANES, 6), (DIAGONAL, 1), (PLANES, 7), (LINES, 3), (PLANES, 8), (SIBLING, 0), (PLANES, 9), (SHARDS, 5), (PLANES, 10),),
    (),
    ((DIAGONAL, 2), (PLANES, 11), (LINES, 4),),
    ((SHARDS, 7), (SIBLING, 1), (LINES, 5),),
    (),
    ((DIAGONAL, 3),),
    ((SHARDS, 9), (SHARDS, 10), (LINES, 6),),
    ((SIBLING, 2), (LINES, 7),),
    (),
    ((DIAGONAL, 4),),
    ((LINES, 8),),
    ((SIBLING, 3), (LINES, 9),),
    (),
    ((DIAGONAL, 6),),
    ((DIAGONAL, 5),),
    ((SIBLING, 4), (LINES, 10),),
    (),
    ((DIAGONAL, 8), (LINES, 11), (SIBLING, 6), (DIAGONAL, 7), (SIBLING, 5),),
    (),
    (),
    ((SIBLING, 8), (DIAGONAL, 9),),
    ((DIAGONAL, 10), (DIAGONAL, 11), (SIBLING, 7),),
    ((SIBLING, 9),),
    (),
    ((SIBLING, 10),),
    (),
    ((SIBLING, 11),),
    (),
    (),
    (),
    (),
)
REDUCE = (
    (),
    (),
    (),
    ((OWN, 8),),
    ((OWN, 4),),
    (),
    ((DIAGONAL, 8), (OWN, 9), (LINES, 8),),
    ((DIAGONAL, 4),),
    ((LINES, 4), (OWN, 5),),
    ((SHARDS, 8), (DIAGONAL, 9),),
    ((LINES, 9), (OWN, 10),),
    ((DIAGONAL, 5),),
    ((LINES, 5), (OWN, 6),),
    ((SHARDS, 4), (DIAGONAL, 10),),
    ((OWN, 11),),
    ((DIAGONAL, 6),),
    ((OWN, 7), (SHARDS, 9),),
    ((LINES, 10), (DONE, 8), (DONE, 4),),
    ((DIAGONAL, 11),),
    (),
    (),
    ((SHARDS, 5), (DIAGONAL, 7), (LINES, 6), (OWN, 3),),
    ((DONE, 9),),
    ((LINES, 11), (DONE, 5),),
    ((LINES, 7), (OWN, 2), (DONE, 10), (DIAGONAL, 3),),
    ((DONE, 6),),
    ((DIAGONAL, 2),),
    ((OWN, 1), (DONE, 11), (LINES, 3),),
    ((LINES, 2), (DONE, 7),),
    ((DIAGONAL, 1),),
    ((OWN, 0), (DONE, 3),),
    ((LINES, 1),),
    ((DIAGONAL, 0), (DONE, 2),),
    ((DONE, 1), (LINES, 0), (DONE, 0),),
)


def nn(left, right):
    return lax.dot_general(left, right, (((1,), (0,)), ((), ())), preferred_element_type=f32)


def nt(left, right):
    return lax.dot_general(left, right, (((1,), (1,)), ((), ())), preferred_element_type=f32)


def tn(left, right):
    return lax.dot_general(left, right, (((0,), (0,)), ((), ())), preferred_element_type=f32)


def tile(index, size):
    if isinstance(index, int):
        return pl.ds(index * size, size)
    return pl.ds(pl.multiple_of(index * size, size), size)


def loop(count, body):
    def step(index, carry):
        body(index)
        return carry

    if count == 1:
        body(0)
    else:
        lax.fori_loop(0, count, step, 0)


def mean_last(values):
    return jnp.sum(values, axis=-1, keepdims=True) * (1.0 / values.shape[-1])


def fold_rows(values):
    return jnp.sum(values.reshape(values.shape[0] // 8, 8, values.shape[1]), axis=0)


def fold_tile(values):
    folded = fold_rows(values)
    return sum(folded[:, c : c + LANES] for c in range(0, folded.shape[1], LANES))


def unit_part(refs, u):
    if u < 3:
        return jnp.concatenate([refs[0][k, :, pl.ds(u * LANES, LANES)] for k in range(3)], axis=1)
    if u == 3:
        return refs[1][...]
    return refs[2 + (u - 4) // 4][:, pl.ds((u % 4) * HALF, HALF)]


def adam_moments(gradient, first_moment, second_moment):
    first_new = BETA_FIRST * first_moment + (1.0 - BETA_FIRST) * gradient
    second_new = BETA_SECOND * second_moment + (1.0 - BETA_SECOND) * gradient * gradient
    direction = (
        first_new
        / (1.0 - BETA_FIRST**STEP)
        / (jnp.sqrt(second_new / (1.0 - BETA_SECOND**STEP)) + ADAM_EPS)
    )
    return (first_new, second_new, direction)


def head_lane():
    return lax.broadcasted_iota(jnp.int32, (1, QUAD), 1) // HEAD


def spread_heads(values):
    lane = head_lane()
    zero = jnp.zeros_like(values)
    return jnp.concatenate([jnp.where(lane == head, values, zero) for head in range(4)], axis=0)


def pick_heads(values, length):
    lane = head_lane()
    result = values[:length]
    for head in range(1, 4):
        result = jnp.where(lane == head, values[head * length : (head + 1) * length], result)
    return result


def lanes(offset, size=LANES):
    if isinstance(offset, int):
        return pl.ds(offset, size)
    return pl.ds(pl.multiple_of(offset, LANES), size)


def pair(ref, rows, offset):
    return jnp.concatenate([ref[rows, lanes(offset)], ref[rows, lanes(HALF + offset)]], axis=1)


def put_pair(ref, rows, offset, values):
    ref[rows, lanes(offset)] = values[:, :LANES]
    ref[rows, lanes(HALF + offset)] = values[:, LANES:]


def main_kernel(
    comm,
    lengths,
    tokens_hbm,
    cot_hbm,
    small,
    w_in,
    w_mid,
    w_up,
    w_down,
    *rest,
):
    if comm:
        *moments_hbm, out_hbm, back_hbm, shard, vectors, norms, probs_hbm = rest[:14]
        rest = rest[14:]
    else:
        whole_hbm, out_hbm, back_hbm, shard, vectors, probs_hbm = rest[:6]
        rest = rest[6:]
    (
        back,
        unit,
        packed,
        context,
        normed,
        inverse,
        first,
        hidden,
        slope,
        own,
        cot,
        flip_a,
        flip_b,
        probs,
        sums,
        up_sums,
        local_sem,
        probs_sem,
        *rest,
    ) = rest
    if comm:
        sib_in, diag_in, line_in, z_in, *rest = rest
        squares, square_in, vec_sum, vec_in, vec_z_in = rest[:5]
        send, recv, rs_send, rs_recv, vec_send, vec_recv, square_send, square_recv, held_sem, shard_sem = rest[5:]
    micro, per_micro = lengths.shape
    chains = micro * per_micro
    length = own.shape[0] // chains
    count = own.shape[0]

    planes = unit.shape[1]
    if comm:
        rank = lax.axis_index("dp")
        core = lax.axis_index("mp")
        z, y, x = rank // 4, (rank // 2) % 2, rank % 2
        mine = pl.ds(pl.multiple_of(core * HALF, HALF), HALF)
        other = pl.ds(pl.multiple_of((1 - core) * HALF, HALF), HALF)

        def device(zz, yy, xx, cc):
            return (zz * 4 + yy * 2 + xx, cc)

        y1, x1 = jnp.where(core == 0, y, 1 - y), jnp.where(core == 0, 1 - x, x)
        y2, x2 = jnp.where(core == 0, 1 - y, y), jnp.where(core == 0, x, 1 - x)
        near = device(z, y1, x1, core)
        next_ = device(z, y2, x2, core)
        sibling = device(z, y, x, 1 - core)

        def plane(step):
            return lax.rem(z + step, planes)

        def plane_back(step):
            return lax.rem(z + planes - step, planes)

        def remote(src, dst, ssem, rsem, target):
            return pltpu.make_async_remote_copy(
                src_ref=src,
                dst_ref=dst,
                send_sem=ssem,
                recv_sem=rsem,
                device_id=target,
                device_id_type=MESH,
            )

        LINE = planes - 1

        def gz(u, step):
            piece = unit.at[u, z, y, x, :, mine]
            return remote(
                piece, piece, send.at[u, step - 1], recv.at[u, step - 1], device(plane(step), y, x, core)
            )

        def gline(u, which):
            piece = unit.at[u, :, y, x, :, mine]
            return remote(
                piece,
                piece,
                send.at[u, LINE + which],
                recv.at[u, LINE + which],
                near if which else next_,
            )

        def gdiag(u):
            piece = unit.at[u, :, y2, x2, :, mine]
            return remote(piece, piece, send.at[u, LINE + 2], recv.at[u, LINE + 2], near)

        def gsib(u):
            piece = unit.at[u, :, :, :, :, mine]
            return remote(piece, piece, send.at[u, LINE + 3], recv.at[u, LINE + 3], sibling)

        def gshard(u):
            piece = unit.at[u, z, y, x, :, mine]
            return remote(piece, piece, send.at[u, LINE], recv.at[u, LINE], next_)

        def gz_next(u, step):
            piece = unit.at[u, z, y2, x2, :, mine]
            sem = LINE + 3 + step
            return remote(piece, piece, send.at[u, sem], recv.at[u, sem], device(plane(step), y, x, core))

        def ag_z(u):
            for step in range(1, planes):
                gz(u, step).start()
            if u in SPLIT_GATHER:
                gshard(u).start()

        def ag_shard(u):
            gshard(u).wait_recv()
            for step in range(1, planes):
                gz_next(u, step).start()

        def ag_line(u):
            for step in range(1, planes):
                gz(u, step).wait_recv()
            if u not in SPLIT_GATHER:
                gline(u, 0).start()
            gline(u, 1).start()

        def ag_diag(u):
            if u in SPLIT_GATHER:
                for step in range(1, planes):
                    gz_next(u, step).wait_recv()
            else:
                gline(u, 0).wait_recv()
            gdiag(u).start()

        def ag_sib(u):
            gline(u, 1).wait_recv()
            gdiag(u).wait_recv()
            gsib(u).start()

        def ag_ready(u):
            gsib(u).wait_recv()

        def ag_sent(u):
            for step in range(1, planes):
                gz(u, step).wait_send()
            if u in SPLIT_GATHER:
                gshard(u).wait_send()
                for step in range(1, planes):
                    gz_next(u, step).wait_send()
            else:
                gline(u, 0).wait_send()
            gline(u, 1).wait_send()
            gdiag(u).wait_send()
            gsib(u).wait_send()

        def slot(u):
            return G_SLOT.get(u, u)

        def rsib(u, place=None):
            place = slot(u) if place is None else place
            return remote(
                unit.at[place, :, :, :, :, other], sib_in.at[u], rs_send.at[u, 0], rs_recv.at[u, 0], sibling
            )

        def rdiag(u):
            return remote(
                unit.at[slot(u), :, 1 - y, 1 - x, :, mine],
                diag_in.at[u],
                rs_send.at[u, 1],
                rs_recv.at[u, 1],
                near,
            )

        def rline(u, which):
            yy, xx = (y2, x2) if which else (y1, x1)
            return remote(
                unit.at[slot(u), :, yy, xx, :, mine],
                line_in.at[u, which],
                rs_send.at[u, 2 + which],
                rs_recv.at[u, 2 + which],
                next_ if which else near,
            )

        def rz(u, step):
            return remote(
                unit.at[slot(u), plane(step), y, x, :, mine],
                z_in.at[u, step - 1],
                rs_send.at[u, 3 + step],
                rs_recv.at[u, 3 + step],
                device(plane(step), y, x, core),
            )

        def rz_next(u, step):
            sem = 3 + planes + step - 1
            return remote(
                unit.at[slot(u), plane(step), y2, x2, :, mine],
                line_in.at[u, 1, step - 1],
                rs_send.at[u, sem],
                rs_recv.at[u, sem],
                device(plane(step), y, x, core),
            )

        def rshard(u):
            return remote(
                unit.at[slot(u), z, y2, x2, :, mine],
                line_in.at[u, 1, planes - 1],
                rs_send.at[u, 3],
                rs_recv.at[u, 3],
                next_,
            )

        def rs_start(u, place=None):
            rsib(u, place).start()

        def rs_own(u):
            rsib(u).wait_recv()

            def add(zz):
                for yy in range(2):
                    for xx in range(2):
                        unit[slot(u), zz, yy, xx, :, mine] = (
                            unit[slot(u), zz, yy, xx, :, mine].astype(f32) + sib_in[u, zz, yy, xx].astype(f32)
                        ).astype(bf16)

            loop(planes, add)
            rdiag(u).start()
            rline(u, 0).start()

        def rs_diag(u):
            rdiag(u).wait_recv()

            def add(zz):
                unit[slot(u), zz, y2, x2, :, mine] = (
                    unit[slot(u), zz, y2, x2, :, mine].astype(f32) + diag_in[u, zz].astype(f32)
                ).astype(bf16)

            loop(planes, add)
            if u in SPLIT_SUMS:
                for step in range(1, planes):
                    rz_next(u, step).start()
            else:
                rline(u, 1).start()

        def rs_shard(u):
            total = unit[slot(u), z, y2, x2, :, mine].astype(f32)
            for step in range(1, planes):
                rz_next(u, step).wait_recv()
                total = total + line_in[u, 1, step - 1].astype(f32)
            unit[slot(u), z, y2, x2, :, mine] = total.astype(bf16)
            rshard(u).start()

        def rs_line(u):
            rline(u, 0).wait_recv()
            if u not in SPLIT_SUMS:
                rline(u, 1).wait_recv()

            def add(zz):
                total = unit[slot(u), zz, y, x, :, mine].astype(f32) + line_in[u, 0, zz].astype(f32)
                if u not in SPLIT_SUMS:
                    total = total + line_in[u, 1, zz].astype(f32)
                unit[slot(u), zz, y, x, :, mine] = total.astype(bf16)

            loop(planes, add)
            for step in range(1, planes):
                rz(u, step).start()

        def rs_done(u):
            total = unit[slot(u), z, y, x, :, mine].astype(f32)
            for step in range(1, planes):
                rz(u, step).wait_recv()
                total = total + z_in[u, step - 1].astype(f32)
            if u in SPLIT_SUMS:
                rshard(u).wait_recv()
                total = total + line_in[u, 1, planes - 1].astype(f32)
            _, _, direction = adam_moments(total, normed[held(0, u)], normed[held(1, u)])
            weight = normed[held(2, u)]
            normed[held(0, u)] = total
            shard_copy(u).start()
            heading = direction + DECAY_RATE * weight
            which = MATRIX_OF[u]
            squares[which] += fold_tile(weight * weight)
            squares[4 + which] += fold_tile(heading * heading)

        def held(which, u):
            rows = normed.shape[0] // 20
            row = (which * UNITS + u) // 2 * rows
            return pl.ds(row, rows), pl.ds((u % 2) * HALF, HALF)

        def held_copies(which):
            matrices = (moments_hbm[:4], moments_hbm[4:], (w_in, w_mid, w_up, w_down))[which]
            copies = []
            for u in range(UNITS):
                rows, cols = held(which, u)
                if u < 3:
                    pairs = [
                        (
                            matrices[0].at[k, :, pl.ds(u * LANES, LANES)],
                            normed.at[rows, pl.ds(cols.start + k * LANES, LANES)],
                        )
                        for k in range(3)
                    ]
                elif u == 3:
                    pairs = [(matrices[1], normed.at[rows, cols])]
                else:
                    piece = matrices[2 + (u - 4) // 4].at[:, pl.ds((u % 4) * HALF, HALF)]
                    pairs = [(piece, normed.at[rows, cols])]
                for source, target in pairs:
                    sem = held_sem.at[which, len(copies)]
                    copies.append(pltpu.make_async_copy(source, target, sem))
            return copies

        def shard_copy(u):
            return pltpu.make_async_copy(normed.at[held(0, u)], shard.at[u], shard_sem.at[u])

        def rs_sent(u):
            rsib(u).wait_send()
            rdiag(u).wait_send()
            rline(u, 0).wait_send()
            if u in SPLIT_SUMS:
                rshard(u).wait_send()
                for step in range(1, planes):
                    rz_next(u, step).wait_send()
            else:
                rline(u, 1).wait_send()
            for step in range(1, planes):
                rz(u, step).wait_send()

    if comm:
        gathers = {
            PLANES: ag_z,
            SHARDS: ag_shard,
            LINES: ag_line,
            DIAGONAL: ag_diag,
            SIBLING: ag_sib,
        }
        sums_of = {
            OWN: rs_own,
            DIAGONAL: rs_diag,
            SHARDS: rs_shard,
            LINES: rs_line,
            DONE: rs_done,
        }
    gather_plan, reduce_plan = iter(GATHER), iter(REDUCE)

    def planned(plan, kinds):
        def run():
            for kind, u in next(plan):
                if comm:
                    kinds[kind](u)

        return run

    kinds = (gathers, sums_of) if comm else ({}, {})
    gather, reduce = planned(gather_plan, kinds[0]), planned(reduce_plan, kinds[1])

    def staged(plan, turns, stages, extra=None):
        sends = [[next(plan) for _ in stages] for _ in range(turns)]
        kinds_here = kinds[0] if plan is gather_plan else kinds[1]

        def turn(i):
            for s, stage in enumerate(stages):
                stage(i)
                for k in range(turns):
                    more = extra.get((k, s)) if extra else None
                    if comm and (sends[k][s] or more):

                        @pl.when(i == k)
                        def _(k=k, s=s, more=more):
                            for kind, u in sends[k][s]:
                                kinds_here[kind](u)
                            if more:
                                more()

        loop(turns, turn)

    def nothing(i):
        pass

    def ready(u):
        if comm:
            ag_ready(u)

    def weights(u):
        return unit[u].reshape(WIDE, WIDE)

    def unit_cols(u, columns):
        return unit[u, :, :, :, :, columns].reshape(WIDE, columns.size)

    own_copy = pltpu.make_async_copy(tokens_hbm, own, local_sem.at[0])
    cot_copy = pltpu.make_async_copy(cot_hbm, cot, local_sem.at[1])
    out_copy = pltpu.make_async_copy(cot, out_hbm, local_sem.at[2])
    back_copy = pltpu.make_async_copy(back, back_hbm, local_sem.at[3])
    if comm:
        weight_copies = held_copies(2)
        for copy in weight_copies:
            copy.start()
    own_copy.start()
    cot_copy.start()

    if comm:
        barrier = pltpu.get_barrier_semaphore()
        around = [
            device(z, yy, xx, cc)
            for yy, xx, cc in (
                (y, x, 1 - core),
                (y, 1 - x, core),
                (1 - y, x, core),
                (1 - y, 1 - x, core),
                (y, 1 - x, 1 - core),
                (1 - y, x, 1 - core),
                (1 - y, 1 - x, 1 - core),
            )
        ]
        greeted = around + [device(plane(step), y, x, core) for step in range(1, planes)]
        for target in greeted:
            pl.semaphore_signal(barrier, inc=1, device_id=target, device_id_type=MESH)
        for copy in weight_copies:
            copy.wait()
        for u in range(UNITS):
            unit[u, z, y, x, :, mine] = normed[held(2, u)].astype(bf16)
        pl.semaphore_wait(barrier, len(greeted))
    else:
        unit_copy = pltpu.make_async_copy(whole_hbm, unit, local_sem.at[4])
        unit_copy.start()
        unit_copy.wait()

    gather()
    sums[...] = jnp.zeros_like(sums)
    up_sums[...] = jnp.zeros_like(up_sums)
    if comm:
        squares[...] = jnp.zeros_like(squares)
    own_copy.wait()

    def fold_vectors():
        target = vec_sum.at[0] if comm else vectors
        target[pl.ds(0, 8), :] = jnp.sum(sums[...], axis=1)
        folded = jnp.sum(up_sums[...], axis=1)
        for u in range(4):
            for c in range(2):
                target[pl.ds(8 + c * 2 + u // 2, 1), pl.ds((u % 2) * HALF, HALF)] = folded[
                    u : u + 1, c * HALF : (c + 1) * HALF
                ]

    if comm:
        place = (y * 2 + x) * 2 + core
        vec_targets = (sibling, device(z, y, 1 - x, core), device(z, 1 - y, x, core))

        def vec_copy(stage):
            return remote(
                vec_sum.at[stage],
                vec_in.at[stage],
                vec_send.at[stage],
                vec_recv.at[stage],
                vec_targets[stage],
            )

        def vec_plane(step):
            return remote(
                vec_sum.at[3],
                vec_z_in.at[z],
                vec_send.at[2 + step],
                vec_recv.at[2 + step],
                device(plane(step), y, x, core),
            )

        def vec_start():
            vec_copy(0).start()

        def vec_step(stage):
            vec_copy(stage).wait_recv()
            vec_sum[stage + 1] = vec_sum[stage] + vec_in[stage]
            if stage < 2:
                vec_copy(stage + 1).start()
            else:
                vec_z_in[z] = vec_sum[3]
                for step in range(1, planes):
                    vec_plane(step).start()

        def vec_done():
            for step in range(1, planes):
                vec_plane(step).wait_recv()
            total = vec_z_in[0]
            for zz in range(1, planes):
                total = total + vec_z_in[zz]
            vectors[...] = total

        def vec_sent():
            for stage in range(3):
                vec_copy(stage).wait_send()
            for step in range(1, planes):
                vec_plane(step).wait_send()

        def square_near(step):
            piece = square_in.at[place]
            return remote(piece, piece, square_send.at[step], square_recv.at[step], around[step])

        def square_far(step):
            piece = square_in.at[8 + z]
            sem = len(around) - 1 + step
            return remote(
                piece, piece, square_send.at[sem], square_recv.at[sem], device(plane(step), y, x, core)
            )

        def exchange_squares():
            square_in[place] = jnp.sum(squares[...], axis=1)
            for step in range(len(around)):
                square_near(step).start()
            for step in range(len(around)):
                square_near(step).wait_recv()
            square_in[8 + z] = jnp.sum(square_in[pl.ds(0, 8)], axis=0)
            for step in range(1, planes):
                square_far(step).start()
            for step in range(1, planes):
                square_far(step).wait_recv()
            total = jnp.sum(square_in[pl.ds(8, planes)], axis=0)
            norms[...] = jnp.broadcast_to(
                jnp.sqrt(jnp.sum(total, axis=1, keepdims=True)), norms.shape
            )
            for step in range(len(around)):
                square_near(step).wait_send()
            for step in range(1, planes):
                square_far(step).wait_send()

    def probs_out(t, chain):
        return pltpu.make_async_copy(probs.at[chain], probs_hbm.at[t], probs_sem.at[chain])

    def probs_back(t, chain):
        return pltpu.make_async_copy(probs_hbm.at[t], probs.at[chain], probs_sem.at[chain])

    position = lax.broadcasted_iota(jnp.int32, (1, length), 1)

    def project(g):
        ready(g)
        bias = jnp.concatenate(
            [
                piece
                for c in range(2)
                for piece in (
                    small[pl.ds(0, 1), lanes(c * HALF + g * LANES)],
                    jnp.zeros((1, LANES), f32),
                    small[pl.ds(1, 1), lanes(c * HALF + g * LANES)],
                )
            ],
            axis=1,
        )
        lane = lax.broadcasted_iota(jnp.int32, (1, WIDE), 1) % HALF
        scale = jnp.where(lane < LANES, HEAD ** (-0.5), 1.0)
        for j in range(3):
            cols = pl.ds(j * QUAD, QUAD)
            part = slice(j * QUAD, (j + 1) * QUAD)
            packed[g, :, cols] = (
                (nn(own[...], unit_cols(g, cols)) + bias[:, part]).astype(bf16).astype(f32)
                * scale[:, part]
            ).astype(bf16)

    def attend(g, chain):
        rows = pl.ds(chain * length, length)
        here = packed.at[g]
        queries = spread_heads(pair(here, rows, 0))
        keys = pair(here, rows, LANES)
        values = pair(here, rows, 2 * LANES)
        limit = lengths[chain // per_micro, chain % per_micro]
        scores = jnp.where(position < limit, nt(queries, keys), MASKED_SCORE)
        peak = jnp.max(scores, axis=1, keepdims=True)
        exponent = jnp.exp(scores - peak)
        total = jnp.sum(exponent, axis=1, keepdims=True)
        low = (exponent * (1.0 / total)).astype(bf16)
        mixed = pick_heads(nn(low, values), length).astype(bf16)
        return rows, low, mixed

    def attend_some(some):
        def stage(g):
            @pl.when(g > 0)
            def _():
                for chain in some:
                    probs_out((g - 1) * chains + chain, chain).wait()

            for chain, (rows, low, mixed) in [(chain, attend(g, chain)) for chain in some]:
                probs[chain, :, pl.ds(0, length)] = low
                put_pair(context, rows, g * LANES, mixed)

            @pl.when(g < 2)
            def _():
                for chain in some:
                    probs_out(g * chains + chain, chain).start()

        return stage

    halves = (range(chains // 2), range(chains // 2, chains))
    staged(gather_plan, 3, [nothing, project] + [attend_some(some) for some in halves])

    gather()
    ready(3)

    def mid(r):
        rows = tile(r, count)
        back[rows, :] = nt(context[rows, :], weights(3))

    loop(1, mid)
    gather()

    def first_norm(r):
        rows = tile(r, BLOCK)
        value = own[rows, :].astype(f32) + back[rows, :] + small[pl.ds(2, 1), :]
        center = value - mean_last(value)
        root = lax.rsqrt(mean_last(center * center) + NORM_EPS)
        scaled = center * root
        normed[rows, :] = scaled
        inverse[rows, :] = root
        first[rows, :] = (scaled * small[pl.ds(3, 1), :] + small[pl.ds(4, 1), :]).astype(bf16)

    loop(count // BLOCK, first_norm)
    gather()

    def up(u):
        ready(4 + u)
        bias = jnp.concatenate(
            [
                small[pl.ds(8 + c * 2 + u // 2, 1), lanes((u % 2) * HALF, HALF)]
                for c in range(2)
            ],
            axis=1,
        )
        for j in range(3):
            cols = pl.ds(j * QUAD, QUAD)
            upper = nn(first[...], unit_cols(4 + u, cols)) + bias[:, j * QUAD : (j + 1) * QUAD]
            share = 0.5 + 0.5 * lax.erf(upper * 0.7071067811865476)
            hidden[u, :, cols] = (upper * share).astype(bf16)
            slope[u, :, cols] = (
                share + upper * (0.3989422804014327 * jnp.exp(-0.5 * upper * upper))
            ).astype(bf16)

    def down(u):
        ready(8 + u)
        back[...] += nt(hidden[u], weights(8 + u))

    staged(gather_plan, 4, [nothing, up])
    back[...] = jnp.zeros_like(back)
    staged(gather_plan, 4, [nothing, down])
    if comm:
        for u in range(UNITS):
            ag_sent(u)
    cot_copy.wait()

    def flip(source, target):
        for j in range(WIDE // LANES):
            cols = pl.ds(j * LANES, LANES)
            target[cols, :] = source[:, cols].T

    def second_norm(r):
        rows = tile(r, BLOCK)
        value = (
            normed[rows, :] * small[pl.ds(3, 1), :]
            + small[pl.ds(4, 1), :]
            + back[rows, :]
            + small[pl.ds(5, 1), :]
        )
        center = value - mean_last(value)
        root = lax.rsqrt(mean_last(center * center) + NORM_EPS)
        scaled = center * root
        upstream = cot[rows, :].astype(f32)
        cot[rows, :] = (scaled * small[pl.ds(6, 1), :] + small[pl.ds(7, 1), :]).astype(bf16)
        gained = upstream * small[pl.ds(6, 1), :]
        grad = (gained - mean_last(gained) - scaled * mean_last(gained * scaled)) * root
        back[rows, :] = grad
        low = grad.astype(bf16)
        own[rows, :] = low
        sums[5] += fold_rows(low.astype(f32))
        sums[6] += fold_rows(upstream * scaled)
        sums[7] += fold_rows(upstream)

    loop(count // BLOCK, second_norm)
    out_copy.start()
    flip(own, flip_a)
    flip(first, flip_b)

    def outer(place, flipped, source):
        part = nn(flipped[...], source[...]).astype(bf16)
        unit[place] = part.reshape(unit.shape[1:])

    def hidden_back(u):
        for j in range(3):
            cols = pl.ds(j * QUAD, QUAD)
            low = (nn(own[...], unit_cols(8 + u, cols)) * slope[u, :, cols].astype(f32)).astype(bf16)
            slope[u, :, cols] = low
            up_sums[u, :, cols] += fold_rows(low.astype(f32))

    def down_sums(u):
        outer(8 + u, flip_a, hidden.at[u])
        if comm:
            rs_start(8 + u, 8 + u)

    def first_part(u):
        back[...] += nt(slope[u], weights(4 + u))

    def up_sums_out(u):
        outer(4 + u, flip_b, slope.at[u])
        if comm:
            rs_start(4 + u, 4 + u)

    staged(reduce_plan, 4, [hidden_back, down_sums, first_part, up_sums_out])

    def first_back(r):
        rows = tile(r, BLOCK)
        upstream = back[rows, :]
        scaled = normed[rows, :]
        gained = upstream * small[pl.ds(3, 1), :]
        grad = (gained - mean_last(gained) - scaled * mean_last(gained * scaled)) * inverse[rows, :]
        back[rows, :] = grad
        low = grad.astype(bf16)
        own[rows, :] = low
        sums[2] += fold_rows(low.astype(f32))
        sums[3] += fold_rows(upstream * scaled)
        sums[4] += fold_rows(upstream)

    loop(count // BLOCK, first_back)
    if comm:
        step_copies = held_copies(0) + held_copies(1) + held_copies(2)
        for copy in step_copies:
            copy.start()
    reduce()
    out_copy.wait()
    flip(own, flip_a)
    if comm:
        for copy in step_copies:
            copy.wait()
    reduce()

    for j in range(3):
        cols = pl.ds(j * QUAD, QUAD)
        cot[:, cols] = nn(own[...], unit_cols(3, cols)).astype(bf16)
    reduce()
    outer(3, flip_a, context)
    if comm:
        rs_start(3)
    own_again = pltpu.make_async_copy(tokens_hbm, own, local_sem.at[0])
    own_again.start()
    reduce()
    own_again.wait()
    flip(own, flip_b)
    reduce()

    def attend_back(g, chain):
        rows = pl.ds(chain * length, length)
        here = packed.at[g]
        queries = spread_heads(pair(here, rows, 0))
        keys = pair(here, rows, LANES)
        values = pair(here, rows, 2 * LANES)
        d_context = spread_heads(pair(cot, rows, g * LANES))
        low = probs[chain, :, pl.ds(0, length)]
        wide = low.astype(f32)
        d_probs = nt(d_context, values)
        inner = jnp.sum(wide * d_probs, axis=1, keepdims=True)
        d_scores = (wide * (d_probs - inner)).astype(bf16)
        d_queries = (pick_heads(nn(d_scores, keys), length) * HEAD ** (-0.5)).astype(bf16)
        d_keys = tn(d_scores, queries).astype(bf16)
        d_values = tn(low, d_context).astype(bf16)
        return rows, d_queries, d_keys, d_values

    def back_some(some):
        def stage(i):
            g = 2 - i
            grads = hidden.at[g]

            @pl.when(g < 2)
            def _():
                for chain in some:
                    probs_back(g * chains + chain, chain).wait()

            results = [attend_back(g, chain) for chain in some]
            for rows, d_queries, d_keys, d_values in results:
                put_pair(grads, rows, 0, d_queries)
                put_pair(grads, rows, LANES, d_keys)
                put_pair(grads, rows, 2 * LANES, d_values)
            for row, place_of in ((0, 1), (1, 3)):
                folded = sum(fold_rows(result[place_of].astype(f32)) for result in results)
                for c in range(2):
                    cols = lanes(c * HALF + g * LANES)
                    sums[row, :, cols] += folded[:, c * LANES : (c + 1) * LANES]

            @pl.when(g > 0)
            def _():
                for chain in some:
                    probs_back((g - 1) * chains + chain, chain).start()

        return stage

    def head_sums(i):
        g = 2 - i
        place = 8 + (i + 1) % 3
        outer(place, flip_b, hidden.at[g])
        if comm:
            rs_start(g, place)

    def vectors_out():
        fold_vectors()
        vec_start()

    def freed(k):
        def run():
            rs_sent(G_SLOT[2 - k])
            if k == 2:
                vectors_out()

        return run

    def tokens_back(i):
        g = 2 - i
        back[...] += nt(hidden[g], weights(g))

    def tokens_out():
        back_copy.start()
        vec_step(2)

    staged(
        reduce_plan,
        3,
        [back_some(some) for some in halves] + [head_sums],
        {(k, 1): freed(k) for k in range(3)} if comm else None,
    )
    staged(
        reduce_plan,
        3,
        [tokens_back],
        {(0, 0): lambda: vec_step(0), (1, 0): lambda: vec_step(1), (2, 0): tokens_out}
        if comm
        else None,
    )
    if not comm:
        fold_vectors()
        back_copy.start()

    if comm:
        reduce()
        vec_done()
        exchange_squares()
        for u in range(UNITS):
            if u not in G_SLOT.values():
                rs_sent(u)
            shard_copy(u).wait()
        vec_sent()
    else:
        whole_out = pltpu.make_async_copy(unit, shard, local_sem.at[4])
        whole_out.start()
        whole_out.wait()
    back_copy.wait()


def run_layer(tokens, lengths, cotangent, weights, moments, small, ranks):
    rows_here = weights[1].shape[0]
    width = small.shape[1]
    flat = tokens.reshape(-1, width)
    count = flat.shape[0]
    chains = lengths.size
    length = tokens.shape[2]
    comm = gathers_inside(ranks, rows_here)
    planes = ranks // 4 if comm else 4
    padded = -(-length // LANES) * LANES
    steps = planes - 1
    unit_shape = (UNITS, planes, 2, 2, width // (planes * 4), WIDE)
    vmem = pl.BlockSpec(memory_space=pltpu.VMEM)
    hbm = pl.BlockSpec(memory_space=pl.ANY)
    operands = [lengths, flat, cotangent.reshape(-1, width), small, *weights]
    in_specs = [pl.BlockSpec(memory_space=pltpu.SMEM), hbm, hbm, vmem] + [hbm] * 4
    if not comm:
        shard = jnp.stack([unit_part(weights, u) for u in range(UNITS)]).astype(bf16)
        whole = lax.all_gather(shard, "dp", axis=1, tiled=True)
        whole = lax.all_gather(whole, "mp", axis=2, tiled=True)
        operands.append(whole.reshape(unit_shape))
        in_specs.append(hbm)
    else:
        operands += moments
        in_specs += [hbm] * 8
    shard_shape = (UNITS, rows_here, HALF)
    out_shape = [
        jax.ShapeDtypeStruct((count, width), bf16),
        jax.ShapeDtypeStruct((count, width), f32),
        jax.ShapeDtypeStruct(shard_shape, f32) if comm else jax.ShapeDtypeStruct(unit_shape, bf16),
        jax.ShapeDtypeStruct(small.shape, f32),
        jax.ShapeDtypeStruct((2 * chains, 4 * length, padded), bf16),
    ]
    out_specs = [hbm, hbm, hbm, vmem, hbm]
    if comm:
        out_shape.insert(4, jax.ShapeDtypeStruct((8, LANES), f32))
        out_specs.insert(4, vmem)
    scratch = [
        pltpu.VMEM((count, width), f32),
        pltpu.VMEM(unit_shape, bf16),
        pltpu.VMEM((3, count, WIDE), bf16),
        pltpu.VMEM((count, width), bf16),
        pltpu.VMEM((count, width), f32),
        pltpu.VMEM((count, 1), f32),
        pltpu.VMEM((count, width), bf16),
        pltpu.VMEM((4, count, WIDE), bf16),
        pltpu.VMEM((4, count, WIDE), bf16),
        pltpu.VMEM((count, width), bf16),
        pltpu.VMEM((count, width), bf16),
        pltpu.VMEM((width, count), bf16),
        pltpu.VMEM((width, count), bf16),
        pltpu.VMEM((chains, 4 * length, padded), bf16),
        pltpu.VMEM((8, 8, width), f32),
        pltpu.VMEM((4, 8, WIDE), f32),
        pltpu.SemaphoreType.DMA((5,)),
        pltpu.SemaphoreType.DMA((chains,)),
    ]
    params = dict(vmem_limit_bytes=64 * 2**20 - 2**16)
    if comm:
        scratch += [
            pltpu.VMEM((UNITS, planes, 2, 2, rows_here, HALF), bf16),
            pltpu.VMEM((UNITS, planes, rows_here, HALF), bf16),
            pltpu.VMEM((UNITS, 2, planes, rows_here, HALF), bf16),
            pltpu.VMEM((UNITS, steps, rows_here, HALF), bf16),
            pltpu.VMEM((8, 8, LANES), f32),
            pltpu.VMEM((8 + planes, 8, LANES), f32),
            pltpu.VMEM((4,) + small.shape, f32),
            pltpu.VMEM((3,) + small.shape, f32),
            pltpu.VMEM((planes,) + small.shape, f32),
            pltpu.SemaphoreType.DMA((UNITS, 2 * steps + 4)),
            pltpu.SemaphoreType.DMA((UNITS, 2 * steps + 4)),
            pltpu.SemaphoreType.DMA((UNITS, 2 * steps + 4)),
            pltpu.SemaphoreType.DMA((UNITS, 2 * steps + 4)),
            pltpu.SemaphoreType.DMA((3 + steps,)),
            pltpu.SemaphoreType.DMA((3 + steps,)),
            pltpu.SemaphoreType.DMA((7 + steps,)),
            pltpu.SemaphoreType.DMA((7 + steps,)),
            pltpu.SemaphoreType.DMA((3, UNITS + 6)),
            pltpu.SemaphoreType.DMA((UNITS,)),
        ]
        params.update(collective_id=0, has_side_effects=True)
    out, back, shard, vectors, *rest = pl.pallas_call(
        functools.partial(main_kernel, comm),
        out_shape=out_shape,
        in_specs=in_specs,
        out_specs=out_specs,
        scratch_shapes=scratch,
        compiler_params=pltpu.CompilerParams(**params),
    )(*operands)
    norms = rest[0] if comm else None
    if not comm:
        summed = shard.reshape(UNITS, width, 2, HALF).astype(f32)
        summed = lax.psum_scatter(summed, "mp", scatter_dimension=2, tiled=True)
        summed = lax.psum_scatter(
            summed.reshape(UNITS, width, HALF), "dp", scatter_dimension=1, tiled=True
        )
        shard = summed
    return out, back, shard, vectors, norms


def gathers_inside(ranks, rows_here):
    return ranks % 4 == 0 and rows_here % 16 == 0


def put_unit(refs, u, values):
    if u < 3:
        for k in range(3):
            refs[0][k, :, pl.ds(u * LANES, LANES)] = values[:, k * LANES : (k + 1) * LANES]
    elif u == 3:
        refs[1][...] = values
    else:
        refs[2 + (u - 4) // 4][:, pl.ds((u % 4) * HALF, HALF)] = values


def step_kernel(*refs):
    out_in, back_in, shard, vectors, norms = refs[:5]
    weights, moments = refs[5:9], refs[9:17]
    small, small_first, small_second = refs[17:20]
    outs = refs[20:-3]
    out_held, back_held, sem = refs[-3:]
    inward = [
        pltpu.make_async_copy(out_in, out_held, sem.at[0]),
        pltpu.make_async_copy(back_in, back_held, sem.at[1]),
    ]
    outward = [
        pltpu.make_async_copy(out_held, outs[0], sem.at[2]),
        pltpu.make_async_copy(back_held, outs[1], sem.at[3]),
    ]
    for copy in inward:
        copy.start()
    grads, firsts, seconds, news, lows = (
        [outs[2 + 5 * m + which] for m in range(4)] for which in range(5)
    )
    for u in range(UNITS):
        if u in (4, 8):
            inward[u // 4 - 1].wait()
            outward[u // 4 - 1].start()
        gradient = shard[u]
        first_new, second_new, direction = adam_moments(
            gradient, unit_part(moments[:4], u), unit_part(moments[4:], u)
        )
        weight = unit_part(weights, u)
        which = MATRIX_OF[u]
        rate = RATE_MATRIX * (norms[which : which + 1, :1] / norms[4 + which : 5 + which, :1])
        renewed = weight - rate * (direction + DECAY_RATE * weight)
        put_unit(grads, u, gradient)
        put_unit(firsts, u, first_new)
        put_unit(seconds, u, second_new)
        put_unit(news, u, renewed)
        put_unit(lows, u, renewed.astype(bf16))
    vector_grad = vectors[...]
    first_new, second_new, direction = adam_moments(vector_grad, small_first[...], small_second[...])
    outs[22][...] = vector_grad
    outs[23][...] = first_new
    outs[24][...] = second_new
    outs[25][...] = small[...] - RATE_VECTOR * direction
    for row in range(2):
        for m in range(4):
            outs[26][pl.ds(row, 1), pl.ds(m, 1)] = norms[4 * row + m : 4 * row + m + 1, :1]
    for copy in outward:
        copy.wait()


def run_step(out, back, shard, vectors, norms, weights, moments, small, small_first, small_second):
    vmem = pl.BlockSpec(memory_space=pltpu.VMEM)
    hbm = pl.BlockSpec(memory_space=pl.ANY)
    out_shape = [jax.ShapeDtypeStruct(out.shape, bf16), jax.ShapeDtypeStruct(back.shape, f32)]
    for weight in weights:
        out_shape += [jax.ShapeDtypeStruct(weight.shape, f32)] * 4
        out_shape += [jax.ShapeDtypeStruct(weight.shape, bf16)]
    out_shape += [jax.ShapeDtypeStruct(small.shape, f32)] * 4
    out_shape += [jax.ShapeDtypeStruct((2, 4), f32)]
    return pl.pallas_call(
        step_kernel,
        out_shape=out_shape,
        in_specs=[hbm, hbm] + [vmem] * 18,
        out_specs=[hbm, hbm] + [vmem] * 25,
        scratch_shapes=[
            pltpu.VMEM(out.shape, bf16),
            pltpu.VMEM(back.shape, f32),
            pltpu.SemaphoreType.DMA((4,)),
        ],
        compiler_params=pltpu.CompilerParams(vmem_limit_bytes=64 * 2**20 - 2**16),
    )(out, back, shard, vectors, norms, *weights, *moments, small, small_first, small_second)


def body(
    ranks,
    tokens,
    lengths,
    cotangent,
    attn_in,
    attn_out,
    ffn_in,
    ffn_out,
    attn_in_first,
    attn_in_second,
    attn_out_first,
    attn_out_second,
    ffn_in_first,
    ffn_in_second,
    ffn_out_first,
    ffn_out_second,
    small,
    small_first,
    small_second,
):
    weights = (attn_in.transpose(1, 0, 2), attn_out.T, ffn_in, ffn_out.T)
    all_moments = (
        attn_in_first.transpose(1, 0, 2),
        attn_out_first.T,
        ffn_in_first,
        ffn_out_first.T,
        attn_in_second.transpose(1, 0, 2),
        attn_out_second.T,
        ffn_in_second,
        ffn_out_second.T,
    )
    output, tokens_grad, shard, vectors, norms = run_layer(
        tokens, lengths, cotangent, weights, all_moments, small, ranks
    )
    if norms is not None:
        results = run_step(
            output,
            tokens_grad,
            shard,
            vectors,
            norms,
            weights,
            all_moments,
            small,
            small_first,
            small_second,
        )
        results = list(results)
        results[0] = results[0].reshape(tokens.shape)
        results[1] = results[1].reshape(tokens.shape)
        for i in range(5):
            results[2 + i] = results[2 + i].transpose(1, 0, 2)
            results[7 + i] = results[7 + i].T
            results[17 + i] = results[17 + i].T
        return tuple(results)
    output, tokens_grad = output.reshape(tokens.shape), tokens_grad.reshape(tokens.shape)
    rows = attn_in.shape[0]
    grad_in = jnp.concatenate([shard[g].reshape(rows, 3, LANES) for g in range(3)], axis=2)
    grad_mid = shard[3].T
    grad_up = jnp.concatenate([shard[4 + u] for u in range(4)], axis=1)
    grad_down = jnp.concatenate([shard[8 + u].T for u in range(4)], axis=0)
    matrices = (
        (attn_in, grad_in, attn_in_first, attn_in_second),
        (attn_out, grad_mid, attn_out_first, attn_out_second),
        (ffn_in, grad_up, ffn_in_first, ffn_in_second),
        (ffn_out, grad_down, ffn_out_first, ffn_out_second),
    )
    moments = [adam_moments(entry[1], entry[2], entry[3]) for entry in matrices]
    headings = [moments[i][2] + DECAY_RATE * matrices[i][0] for i in range(4)]
    weight_squares = jnp.stack([jnp.sum(entry[0] * entry[0]) for entry in matrices])
    step_squares = jnp.stack([jnp.sum(heading * heading) for heading in headings])
    vector_grad, weight_sums, step_sums = lax.psum(
        (vectors, weight_squares, step_squares), ("dp", "mp")
    )
    weight_norms = jnp.sqrt(weight_sums)
    step_norms = jnp.sqrt(step_sums)
    results = [output, tokens_grad]
    for i in range(4):
        weight = matrices[i][0]
        renewed = weight - RATE_MATRIX * (weight_norms[i] / step_norms[i]) * headings[i]
        results.extend(
            [matrices[i][1], moments[i][0], moments[i][1], renewed, renewed.astype(bf16)]
        )
    small_first_new, small_second_new, small_direction = adam_moments(
        vector_grad, small_first, small_second
    )
    small_new = small - RATE_VECTOR * small_direction
    results.extend(
        [
            vector_grad,
            small_first_new,
            small_second_new,
            small_new,
            jnp.stack((weight_norms, step_norms)),
        ]
    )
    return tuple(results)


def solution(mesh):
    chains = P(None, ("dp", "mp"), None, None)
    rows_three = P("dp", None, "mp")
    rows_two = P("dp", "mp")
    columns = P("mp", "dp")
    whole = P()
    return jax.shard_map(
        functools.partial(body, mesh.shape["dp"]),
        mesh=mesh,
        in_specs=(
            chains,
            P(None, ("dp", "mp")),
            chains,
            rows_three,
            columns,
            rows_two,
            columns,
            rows_three,
            rows_three,
            columns,
            columns,
            rows_two,
            rows_two,
            columns,
            columns,
            whole,
            whole,
            whole,
        ),
        out_specs=(
            (chains, chains)
            + (rows_three,) * 5
            + (columns,) * 5
            + (rows_two,) * 5
            + (columns,) * 5
            + (whole,) * 5
        ),
        check_vma=False,
    )
```

profile of v0, /device:TPU:0, one launch (start us, length us, event | category | flops | bytes accessed | tf_op | source)
XLA Modules:
  0.0 183.9 jit_solution(16682223885832334409)
XLA Ops:
  0.7 175.0 %shard_map.385 = (bf16[960,768]{1,0:T(8,128)(2,1)}, f32[960,768]{1,0:T(8,128)}, f32[12,48,384]{2,1,0:T(8,128)}, f32[12,768]{1,0:T(8,128)}, f32[8,128]{1,0:T(8,128)}, /*index=5*/bf16[12,640,256]{2,1,0:T(8,128)(2,1)}) custom-call(s32[2,3]{1,0:T(2,128)} %lengths.1, bf16[960,768]{1,0:T(8,128)(2,1)} %bitcast.28, bf16[960,768]{1,0:T(8,128)(2,1)} %bitcast.29, ...), custom_call_target="tpu_custom_call" | custom-call | tf_op jit(solution)/shard_map/pallas_call | solution.py:1137
  175.6 8.1 %shard_map.386 = (bf16[960,768]{1,0:T(8,128)(2,1)}, f32[960,768]{1,0:T(8,128)}, f32[3,48,384]{2,1,0:T(8,128)}, f32[3,48,384]{2,1,0:T(8,128)}, f32[3,48,384]{2,1,...) custom-call(bf16[960,768]{1,0:T(8,128)(2,1)} %get-tuple-element.59.r, ...), custom_call_target="tpu_custom_call" | custom-call | tf_op jit(solution)/shard_map/pallas_call | solution.py:1228
where the time goes:
time: 184 us
  Pallas kernels  183 us (99%)
    pallas_call x1, Pallas kernels, run_layer(): pl.pallas_call(functools.partial(main_kernel, comm), out_shape=out_shape,...  175 us
    pallas_call x1, Pallas kernels, run_step(): pl.pallas_call(step_kernel, out_shape=out_shape, in_specs=[hbm, hbm] + [v...  8.07 us

commit v1 on v0

--- a/solution.py
+++ b/solution.py
@@ -637,6 +637,12 @@
     if comm:
         squares[...] = jnp.zeros_like(squares)
     own_copy.wait()
+    cot_copy.wait()
+
+    def shift_sums(r):
+        sums[7] += fold_rows(cot[tile(r, BLOCK), :].astype(f32))
+
+    loop(count // BLOCK, shift_sums)
 
     def fold_vectors():
         target = vec_sum.at[0] if comm else vectors
@@ -814,7 +820,9 @@
         scaled = center * root
         normed[rows, :] = scaled
         inverse[rows, :] = root
-        first[rows, :] = (scaled * small[pl.ds(3, 1), :] + small[pl.ds(4, 1), :]).astype(bf16)
+        shifted = scaled * small[pl.ds(3, 1), :] + small[pl.ds(4, 1), :]
+        first[rows, :] = shifted.astype(bf16)
+        back[rows, :] = shifted + small[pl.ds(5, 1), :]
 
     loop(count // BLOCK, first_norm)
     gather()
@@ -842,13 +850,10 @@
         back[...] += nt(hidden[u], weights(8 + u))
 
     staged(gather_plan, 4, [nothing, up])
-    back[...] = jnp.zeros_like(back)
     staged(gather_plan, 4, [nothing, down])
     if comm:
         for u in range(UNITS):
             ag_sent(u)
-    cot_copy.wait()
-
     def flip(source, target):
         for j in range(WIDE // LANES):
             cols = pl.ds(j * LANES, LANES)
@@ -856,12 +861,7 @@
 
     def second_norm(r):
         rows = tile(r, BLOCK)
-        value = (
-            normed[rows, :] * small[pl.ds(3, 1), :]
-            + small[pl.ds(4, 1), :]
-            + back[rows, :]
-            + small[pl.ds(5, 1), :]
-        )
+        value = back[rows, :]
         center = value - mean_last(value)
         root = lax.rsqrt(mean_last(center * center) + NORM_EPS)
         scaled = center * root
@@ -874,7 +874,6 @@
         own[rows, :] = low
         sums[5] += fold_rows(low.astype(f32))
         sums[6] += fold_rows(upstream * scaled)
-        sums[7] += fold_rows(upstream)
 
     loop(count // BLOCK, second_norm)
     out_copy.start()

time: 184 us -> 184 us (level)
  no operation moved by 1% of the time
where the time goes in v1:
time: 184 us
  Pallas kernels  183 us (99%)
    pallas_call x1, Pallas kernels, run_layer(): pl.pallas_call(functools.partial(main_kernel, comm), out_shape=out_shape,...  175 us
    pallas_call x1, Pallas kernels, run_step(): pl.pallas_call(step_kernel, out_shape=out_shape, in_specs=[hbm, hbm] + [v...  8.07 us

profile of v1, /device:TPU:0, one launch (start us, length us, event | category | flops | bytes accessed | tf_op | source)
XLA Modules:
  0.0 184.0 jit_solution(2158386206043330453)
XLA Ops:
  0.7 175.1 %shard_map.385 = (bf16[960,768]{1,0:T(8,128)(2,1)}, f32[960,768]{1,0:T(8,128)}, f32[12,48,384]{2,1,0:T(8,128)}, f32[12,768]{1,0:T(8,128)}, f32[8,128]{1,0:T(8,128)}, /*index=5*/bf16[12,640,256]{2,1,0:T(8,128)(2,1)}) custom-call(s32[2,3]{1,0:T(2,128)} %lengths.1, bf16[960,768]{1,0:T(8,128)(2,1)} %bitcast.28, bf16[960,768]{1,0:T(8,128)(2,1)} %bitcast.29, ...), custom_call_target="tpu_custom_call" | custom-call | tf_op jit(solution)/shard_map/pallas_call | solution.py:1136
  175.7 8.1 %shard_map.386 = (bf16[960,768]{1,0:T(8,128)(2,1)}, f32[960,768]{1,0:T(8,128)}, f32[3,48,384]{2,1,0:T(8,128)}, f32[3,48,384]{2,1,0:T(8,128)}, f32[3,48,384]{2,1,...) custom-call(bf16[960,768]{1,0:T(8,128)(2,1)} %get-tuple-element.59.r, ...), custom_call_target="tpu_custom_call" | custom-call | tf_op jit(solution)/shard_map/pallas_call | solution.py:1227
